TPU v7x, 32 devices: a whole 2x2x4 slice. The times are simulated.
32 devices in a mesh: lat: 4 (over y, x), lon: 2 (over core), ch: 4 (over z).
Axes of the slice: x: 2, y: 2, z: 4, core: 2. Of those that a mesh axis runs over, the one named last changes fastest.
Arguments:
- features: bfloat16 [1, 64, 128, 256], P(None, 'lat', 'lon'), may hold values from -6 to 6
- w_first: bfloat16 [5, 5, 256, 256], P(None, None, None, 'ch'), may hold values from -0.078125 to 0.078125
- bias_first: float32 [256], P('ch'), may hold values from -3 to 3
- w_second: bfloat16 [5, 5, 256, 256], P(None, None, 'ch'), may hold values from -0.109375 to 0.109375
- bias_second: float32 [256], replicated, may hold values from -3 to 3
- norm_gain: float32 [256], replicated, may hold values from 0.25 to 1.75
- norm_shift: float32 [256], replicated, may hold values from -3 to 3
- w_down: bfloat16 [2, 2, 256, 256], P(None, None, None, 'ch'), may hold values from -0.1875 to 0.1875
- bias_down: float32 [256], P('ch'), may hold values from -3 to 3
Outputs:
- downsampled: bfloat16 [1, 32, 64, 256], P(None, 'lat', 'lon', 'ch')
All inputs are finite; a program needn't handle non-finite values.
Results may differ from a plain program's by a relative error of at most 0.011.
Values may be sent and summed in bfloat16 or wider, within the bound.
A program may use at most 64 MiB of HBM per device.

v0:
```python
import jax
import jax.numpy as jnp
from jax import lax
from jax.sharding import PartitionSpec as P


def padded_2(block, sides, width):
    for axis, dim in sides:
        count = lax.axis_size(axis)
        forward = [(i, i + 1) for i in range(count - 1)]
        backward = [(target, source) for source, target in forward]
        low = lax.ppermute(
            lax.slice_in_dim(block, block.shape[dim] - width, None, axis=dim), axis, forward
        )
        high = lax.ppermute(lax.slice_in_dim(block, 0, width, axis=dim), axis, backward)
        block = jnp.concatenate([low, block, high], axis=dim)
    return block


def conv_taps(padded, kernel, dilation, rows, cols):
    total = None
    for row_tap in range(5):
        for col_tap in range(5):
            window = padded[
                :,
                row_tap * dilation : row_tap * dilation + rows,
                col_tap * dilation : col_tap * dilation + cols,
                :,
            ]
            term = jnp.einsum(
                "bhwc,cd->bhwd",
                window,
                kernel[row_tap, col_tap],
                preferred_element_type=jnp.float32,
            )
            total = term if total is None else total + term
    return total


def shrink(normed, kernel):
    batch, rows, cols, width = normed.shape
    blocks = normed.reshape(batch, rows // 2, 2, cols // 2, 2, width)
    return jnp.einsum("bhiwjc,ijcd->bhwd", blocks, kernel, preferred_element_type=jnp.float32)


def normalize(mixed, total, square_total, width, norm_gain, norm_shift):
    mean = total[..., None] / width
    variance = square_total[..., None] / width - mean * mean
    return ((mixed - mean) * lax.rsqrt(variance + 1e-05) * norm_gain + norm_shift).astype(
        jnp.bfloat16
    )


def body(
    features, w_first, bias_first, w_second, bias_second, norm_gain, norm_shift, w_down, bias_down
):
    batch, rows, cols, width = features.shape
    padded = padded_2(features, (("lat", 1), ("lon", 2)), 2)
    hidden = jax.nn.gelu(conv_taps(padded, w_first, 1, rows, cols) + bias_first).astype(
        jnp.bfloat16
    )
    widened = padded_2(hidden, (("lat", 1), ("lon", 2)), 4)
    partial_value = conv_taps(widened, w_second, 2, rows, cols)
    share = w_second.shape[2]
    offset = lax.axis_index("ch") * share
    summed = lax.psum_scatter(
        partial_value.astype(jnp.bfloat16), "ch", scatter_dimension=3, tiled=True
    ).astype(jnp.float32)
    own_input = lax.dynamic_slice_in_dim(features, offset, share, 3).astype(jnp.float32)
    mixed = own_input + summed + lax.dynamic_slice_in_dim(bias_second, offset, share, 0)
    total, square_total = lax.psum((jnp.sum(mixed, axis=3), jnp.sum(mixed * mixed, axis=3)), "ch")
    normed = normalize(
        mixed,
        total,
        square_total,
        width,
        lax.dynamic_slice_in_dim(norm_gain, offset, share, 0),
        lax.dynamic_slice_in_dim(norm_shift, offset, share, 0),
    )
    result = shrink(lax.all_gather(normed, "ch", axis=3, tiled=True), w_down)
    return (result + bias_down).astype(jnp.bfloat16)


def solution(mesh):
    placed = (
        P(None, "lat", "lon", None),
        P(None, None, None, "ch"),
        P("ch"),
        P(None, None, "ch", None),
        P(),
        P(),
        P(),
        P(None, None, None, "ch"),
        P("ch"),
    )
    return jax.shard_map(
        body, mesh=mesh, in_specs=placed, out_specs=P(None, "lat", "lon", "ch"), check_vma=False
    )
```

profile of v0, /device:TPU:0, one launch (start us, length us, event | category | flops | bytes accessed | tf_op | source)
XLA Modules:
  0.0 123.0 jit_solution(14867023866999693696)
XLA Ops:
  6.5 0.9 fusion.299
  7.5 4.8 %collective-permute-start = (bf16[1,2,64,256]{3,2,1,0:T(8,128)(2,1)S(1)}, bf16[1,2,64,256]{3,2,1,0:T(8,128)(2,1)S(1)}, u32[]{:S(2)}, u32[]{:S(2)}) collective-permute-start(bf16[1,2,64,256]{3,2,1,0:T(8,128)(2,1)S(1)} %get-tuple-element.15), channel_id=1, source_target_pairs={{0,8},{8,16},{16,24},{1,9},{9,17},{17,25},{2,10},{10,18},{18,26},{... | collective-permute-start | bytes 196616 | tf_op jit(solution)/shard_map/ppermute | solution.py:12
  12.3 1.4 %collective-permute-start.1 = (bf16[1,2,64,256]{3,2,1,0:T(8,128)(2,1)S(1)}, bf16[1,2,64,256]{3,2,1,0:T(8,128)(2,1)S(1)}, u32[]{:S(2)}, u32[]{:S(2)}) collective-permute-start(bf16[1,2,64,256]{3,2,1,0:T(8,128)(2,1)S(1)} %get-tuple-element.14), channel_id=1, source_target_pairs={{8,0},{16,8},{24,16},{9,1},{17,9},{25,17},{10,2},{18,10},{26,18},{... | collective-permute-start | bytes 196616 | tf_op jit(solution)/shard_map/ppermute | solution.py:15
  13.8 1.3 %fusion.135 = f32[16,64,64]{2,1,0:T(8,128)S(1)} fusion(bf16[1,16,64,256]{3,2,1,0:T(8,128)(2,1)} %param.9, bf16[5,5,256,64]{2,3,1,0:T(8,128)(2,1)} %param.10), kind=kOutput, calls=%fused_computation.167 | convolution fusion | flops 33554432 | bytes 819200 | tf_op jit(solution)/shard_map/bhwc,cd->bhwd/dot_general | solution.py:30
  15.3 1.0 copy-done.3
  16.8 1.8 %collective-permute-done.1 = bf16[1,2,64,256]{3,2,1,0:T(8,128)(2,1)S(1)} collective-permute-done((bf16[1,2,64,256]{3,2,1,0:T(8,128)(2,1)S(1)}, bf16[1,2,64,256]{3,2,1,0:T(8,128)(2,1)S(1)}, u32[]{:S(2)}, u32[]{:S(2)}) %collective-permute-start.1) | collective-permute-done | bytes 65568 | tf_op jit(solution)/shard_map/ppermute | solution.py:15
  18.7 1.3 %collective-permute-start.2 = (bf16[1,20,2,256]{3,2,1,0:T(2,128)(2,1)S(1)}, bf16[1,20,2,256]{3,2,1,0:T(2,128)(2,1)S(1)}, u32[]{:S(2)}, u32[]{:S(2)}) collective-permute-start(bf16[1,20,2,256]{3,2,1,0:T(2,128)(2,1)S(1)} %get-tuple-element.9), channel_id=1, source_target_pairs={{0,4},{1,5},{2,6},{3,7},{8,12},{9,13},{10,14},{11,15},{16,20},{17,... | collective-permute-start | bytes 61448 | tf_op jit(solution)/shard_map/ppermute | solution.py:12
  20.5 1.3 %collective-permute-start.3 = (bf16[1,20,2,256]{3,2,1,0:T(2,128)(2,1)S(1)}, bf16[1,20,2,256]{3,2,1,0:T(2,128)(2,1)S(1)}, u32[]{:S(2)}, u32[]{:S(2)}) collective-permute-start(bf16[1,20,2,256]{3,2,1,0:T(2,128)(2,1)S(1)} %get-tuple-element.10), channel_id=1, source_target_pairs={{4,0},{5,1},{6,2},{7,3},{12,8},{13,9},{14,10},{15,11},{20,16},{21,... | collective-permute-start | bytes 61448 | tf_op jit(solution)/shard_map/ppermute | solution.py:15
  22.8 0.9 collective-permute-done.3
  28.9 0.6 fusion.35
  29.5 4.3 %collective-permute-start.4 = (bf16[1,4,64,64]{3,2,1,0:T(8,128)(2,1)S(1)}, bf16[1,4,64,64]{3,2,1,0:T(8,128)(2,1)S(1)}, u32[]{:S(2)}, u32[]{:S(2)}) collective-permute-start(bf16[1,4,64,64]{3,2,1,0:T(8,128)(2,1)S(1)} %get-tuple-element.20), channel_id=1, source_target_pairs={{0,8},{8,16},{16,24},{1,9},{9,17},{17,25},{2,10},{10,18},{18,26},{... | collective-permute-start | bytes 98312 | tf_op jit(solution)/shard_map/ppermute | solution.py:12
  33.8 1.4 %collective-permute-start.5 = (bf16[1,4,64,64]{3,2,1,0:T(8,128)(2,1)S(1)}, bf16[1,4,64,64]{3,2,1,0:T(8,128)(2,1)S(1)}, u32[]{:S(2)}, u32[]{:S(2)}) collective-permute-start(bf16[1,4,64,64]{3,2,1,0:T(8,128)(2,1)S(1)} %get-tuple-element.21), channel_id=1, source_target_pairs={{8,0},{16,8},{24,16},{9,1},{17,9},{25,17},{10,2},{18,10},{26,18},{... | collective-permute-start | bytes 98312 | tf_op jit(solution)/shard_map/ppermute | solution.py:15
  35.3 0.4 collective-permute-done.4
  35.7 4.4 %collective-permute-done.5 = bf16[1,4,64,64]{3,2,1,0:T(8,128)(2,1)S(1)} collective-permute-done((bf16[1,4,64,64]{3,2,1,0:T(8,128)(2,1)S(1)}, bf16[1,4,64,64]{3,2,1,0:T(8,128)(2,1)S(1)}, u32[]{:S(2)}, u32[]{:S(2)}) %collective-permute-start.5) | collective-permute-done | bytes 32800 | tf_op jit(solution)/shard_map/ppermute | solution.py:15
  40.2 1.3 %collective-permute-start.6 = (bf16[1,24,4,64]{3,2,1,0:T(4,128)(2,1)S(1)}, bf16[1,24,4,64]{3,2,1,0:T(4,128)(2,1)S(1)}, u32[]{:S(2)}, u32[]{:S(2)}) collective-permute-start(bf16[1,24,4,64]{3,2,1,0:T(4,128)(2,1)S(1)} %get-tuple-element.18), channel_id=1, source_target_pairs={{0,4},{1,5},{2,6},{3,7},{8,12},{9,13},{10,14},{11,15},{16,20},{17,... | collective-permute-start | bytes 36872 | tf_op jit(solution)/shard_map/ppermute | solution.py:12
  41.5 1.5 %collective-permute-start.7 = (bf16[1,24,4,64]{3,2,1,0:T(4,128)(2,1)S(1)}, bf16[1,24,4,64]{3,2,1,0:T(4,128)(2,1)S(1)}, u32[]{:S(2)}, u32[]{:S(2)}) collective-permute-start(bf16[1,24,4,64]{3,2,1,0:T(4,128)(2,1)S(1)} %get-tuple-element.19), channel_id=1, source_target_pairs={{4,0},{5,1},{6,2},{7,3},{12,8},{13,9},{14,10},{15,11},{20,16},{21,... | collective-permute-start | bytes 36872 | tf_op jit(solution)/shard_map/ppermute | solution.py:15
  42.9 1.6 %collective-permute-done.7 = bf16[1,24,4,64]{3,2,1,0:T(4,128)(2,1)S(1)} collective-permute-done((bf16[1,24,4,64]{3,2,1,0:T(4,128)(2,1)S(1)}, bf16[1,24,4,64]{3,2,1,0:T(4,128)(2,1)S(1)}, u32[]{:S(2)}, u32[]{:S(2)}) %collective-permute-start.7) | collective-permute-done | bytes 12320 | tf_op jit(solution)/shard_map/ppermute | solution.py:15
  47.3 0.4 fusion.1
  52.0 1.0 copy.18
  53.0 1.5 %reshape.419 = bf16[256,1024]{1,0:T(8,128)(2,1)} reshape(bf16[256,1,16,64]{3,2,1,0:T(8,128)(2,1)S(1)} %bitcast.441) | data formatting | bytes 1048576
  54.6 0.7 copy-done.5
  55.3 0.6 copy-done.6
  56.0 0.6 copy-done.7
  56.7 20.2 %reduce-scatter.4.cloned.1.call-done = bf16[64,1024]{1,0:T(8,128)(2,1)} async-done(((bf16[256,1024]{1,0:T(8,128)(2,1)}), bf16[64,1024]{1,0:T(8,128)(2,1)}) %reduce-scatter.4.cloned.1.call-update) | async-done | bytes 131088
  76.9 1.1 reshape.420
  78.3 0.5 fusion.137
  78.8 15.8 %all-reduce = (f32[1,16,64]{2,1,0:T(8,128)S(1)}, f32[1,16,64]{2,1,0:T(8,128)S(1)}) all-reduce(f32[1,16,64]{2,1,0:T(8,128)S(1)} %bitcast.444, f32[1,16,64]{2,1,0:T(8,128)S(1)} %bitcast.443), channel_id=1, replica_groups=mesh['lat'=4,'lon'=2,'ch'=4] {'ch'}, use_global_device_ids=true, to_apply=%region_4.0 | all-reduce | flops 2048 | bytes 16384 | tf_op jit(solution)/shard_map/psum | solution.py:71
  94.6 0.4 add_convert_fusion
  95.3 18.5 %all_gather.3 = bf16[1,16,64,256]{2,1,0,3:T(8,128)(2,1)S(1)} all-gather(bf16[1,16,64,64]{2,1,0,3:T(8,128)(2,1)S(1)} %copy.12), channel_id=1, replica_groups=mesh['lat'=4,'lon'=2,'ch'=4] {'ch'}, dimensions={3}, use_global_device_ids=true | all-gather | bytes 655360 | tf_op jit(solution)/shard_map/all_gather | solution.py:80
  113.8 0.8 copy.13
  114.9 0.4 copy-done.8
  115.3 0.9 fusion.27
  (80 shorter events, 15.3 us)
Async XLA Ops:
  6.5 108.3 %copy-start = (bf16[2,2,256,64]{2,3,1,0:T(8,128)(2,1)S(1)}, bf16[2,2,256,64]{2,3,1,0:T(8,128)(2,1)}, u32[]{:S(2)}) copy-start(bf16[2,2,256,64]{2,3,1,0:T(8,128)(2,1)} %param.16) | copy-start | bytes 393220
  6.5 70.3 %reduce-scatter.4.cloned.1.call-start = ((), (), s32[]{:S(2)}) async-start(), calls=%async_computation.1 | async-start | bytes 655360
  7.5 7.6 %collective-permute-start = (bf16[1,2,64,256]{3,2,1,0:T(8,128)(2,1)S(1)}, bf16[1,2,64,256]{3,2,1,0:T(8,128)(2,1)S(1)}, u32[]{:S(2)}, u32[]{:S(2)}) collective-permute-start(bf16[1,2,64,256]{3,2,1,0:T(8,128)(2,1)S(1)} %get-tuple-element.15), channel_id=1, source_target_pairs={{0,8},{8,16},{16,24},{1,9},{9,17},{17,25},{2,10},{10,18},{18,26},{... | collective-permute-start | bytes 196616 | tf_op jit(solution)/shard_map/ppermute | solution.py:12
  12.3 2.8 %copy-start.1 = (bf16[1,16,64,256]{3,2,1,0:T(8,128)(2,1)S(1)}, bf16[1,16,64,256]{3,2,1,0:T(8,128)(2,1)}, u32[]{:S(2)}) copy-start(bf16[1,16,64,256]{3,2,1,0:T(8,128)(2,1)} %param.9) | copy-start | bytes 1572868
  12.3 6.3 %collective-permute-start.1 = (bf16[1,2,64,256]{3,2,1,0:T(8,128)(2,1)S(1)}, bf16[1,2,64,256]{3,2,1,0:T(8,128)(2,1)S(1)}, u32[]{:S(2)}, u32[]{:S(2)}) collective-permute-start(bf16[1,2,64,256]{3,2,1,0:T(8,128)(2,1)S(1)} %get-tuple-element.14), channel_id=1, source_target_pairs={{8,0},{16,8},{24,16},{9,1},{17,9},{25,17},{10,2},{18,10},{26,18},{... | collective-permute-start | bytes 196616 | tf_op jit(solution)/shard_map/ppermute | solution.py:15
  15.1 1.1 copy-start.3
  18.7 3.2 %collective-permute-start.2 = (bf16[1,20,2,256]{3,2,1,0:T(2,128)(2,1)S(1)}, bf16[1,20,2,256]{3,2,1,0:T(2,128)(2,1)S(1)}, u32[]{:S(2)}, u32[]{:S(2)}) collective-permute-start(bf16[1,20,2,256]{3,2,1,0:T(2,128)(2,1)S(1)} %get-tuple-element.9), channel_id=1, source_target_pairs={{0,4},{1,5},{2,6},{3,7},{8,12},{9,13},{10,14},{11,15},{16,20},{17,... | collective-permute-start | bytes 61448 | tf_op jit(solution)/shard_map/ppermute | solution.py:12
  20.5 3.1 %collective-permute-start.3 = (bf16[1,20,2,256]{3,2,1,0:T(2,128)(2,1)S(1)}, bf16[1,20,2,256]{3,2,1,0:T(2,128)(2,1)S(1)}, u32[]{:S(2)}, u32[]{:S(2)}) collective-permute-start(bf16[1,20,2,256]{3,2,1,0:T(2,128)(2,1)S(1)} %get-tuple-element.10), channel_id=1, source_target_pairs={{4,0},{5,1},{6,2},{7,3},{12,8},{13,9},{14,10},{15,11},{20,16},{21,... | collective-permute-start | bytes 61448 | tf_op jit(solution)/shard_map/ppermute | solution.py:15
  28.2 0.7 copy-start.4
  29.5 6.2 %collective-permute-start.4 = (bf16[1,4,64,64]{3,2,1,0:T(8,128)(2,1)S(1)}, bf16[1,4,64,64]{3,2,1,0:T(8,128)(2,1)S(1)}, u32[]{:S(2)}, u32[]{:S(2)}) collective-permute-start(bf16[1,4,64,64]{3,2,1,0:T(8,128)(2,1)S(1)} %get-tuple-element.20), channel_id=1, source_target_pairs={{0,8},{8,16},{16,24},{1,9},{9,17},{17,25},{2,10},{10,18},{18,26},{... | collective-permute-start | bytes 98312 | tf_op jit(solution)/shard_map/ppermute | solution.py:12
  33.8 10.9 %copy-start.2 = (bf16[5,5,64,256]{3,2,1,0:T(8,128)(2,1)S(1)}, bf16[5,5,64,256]{3,2,1,0:T(8,128)(2,1)}, u32[]{:S(2)}) copy-start(bf16[5,5,64,256]{3,2,1,0:T(8,128)(2,1)} %param.12) | copy-start | bytes 2457604
  33.8 6.3 %collective-permute-start.5 = (bf16[1,4,64,64]{3,2,1,0:T(8,128)(2,1)S(1)}, bf16[1,4,64,64]{3,2,1,0:T(8,128)(2,1)S(1)}, u32[]{:S(2)}, u32[]{:S(2)}) collective-permute-start(bf16[1,4,64,64]{3,2,1,0:T(8,128)(2,1)S(1)} %get-tuple-element.21), channel_id=1, source_target_pairs={{8,0},{16,8},{24,16},{9,1},{17,9},{25,17},{10,2},{18,10},{26,18},{... | collective-permute-start | bytes 98312 | tf_op jit(solution)/shard_map/ppermute | solution.py:15
  40.2 2.8 %collective-permute-start.6 = (bf16[1,24,4,64]{3,2,1,0:T(4,128)(2,1)S(1)}, bf16[1,24,4,64]{3,2,1,0:T(4,128)(2,1)S(1)}, u32[]{:S(2)}, u32[]{:S(2)}) collective-permute-start(bf16[1,24,4,64]{3,2,1,0:T(4,128)(2,1)S(1)} %get-tuple-element.18), channel_id=1, source_target_pairs={{0,4},{1,5},{2,6},{3,7},{8,12},{9,13},{10,14},{11,15},{16,20},{17,... | collective-permute-start | bytes 36872 | tf_op jit(solution)/shard_map/ppermute | solution.py:12
  41.5 3.1 %collective-permute-start.7 = (bf16[1,24,4,64]{3,2,1,0:T(4,128)(2,1)S(1)}, bf16[1,24,4,64]{3,2,1,0:T(4,128)(2,1)S(1)}, u32[]{:S(2)}, u32[]{:S(2)}) collective-permute-start(bf16[1,24,4,64]{3,2,1,0:T(4,128)(2,1)S(1)} %get-tuple-element.19), channel_id=1, source_target_pairs={{4,0},{5,1},{6,2},{7,3},{12,8},{13,9},{14,10},{15,11},{20,16},{21,... | collective-permute-start | bytes 36872 | tf_op jit(solution)/shard_map/ppermute | solution.py:15
  54.5 0.7 copy-start.5
  55.2 0.7 copy-start.6
  55.9 0.7 copy-start.7
  114.6 0.7 copy-start.8
Sparse Core Ops, SparseCore 0:
  54.7 22.1 reduce-scatter.3
where the time goes:
time: 124 us; the launch traced here: 123 us
  blocking collectives  34.3 us (28%)
  waiting for transfers between devices  29.4 us (24%)
  starting transfers between devices  17.3 us (14%)
  matrix products  16.7 us (13%)
  between operations  14 us (11%)
  local copies, waits for them, and re-layouts  10.2 us (8%)
    unnamed x2, waiting for transfers between devices  20.2 us
    all_gather x1, blocking collectives, body(): result = shrink(lax.all_gather(normed, 'ch', axis=3, tiled=True), w_down)  18.5 us
    psum x1, blocking collectives, body(): lax.psum((jnp.sum(mixed, axis=3), jnp.sum(mixed * mixed, axis=3)), 'ch')  15.8 us
    dot_general x50, matrix products, conv_taps(): jnp.einsum('bhwc,cd->bhwd', window, kernel[row_tap, col_tap], preferred_e...  15.8 us
    ppermute x4, starting transfers between devices, padded_2(): lax.ppermute(lax.slice_in_dim(block, block.shape[dim] - width, None, axis...  11.7 us
    ppermute x4, waiting for transfers between devices, padded_2(): lax.ppermute(lax.slice_in_dim(block, 0, width, axis=dim), axis, backward)  8.68 us
    unnamed x23, local copies, waits for them, and re-layouts  7.54 us
    ppermute x4, starting transfers between devices, padded_2(): lax.ppermute(lax.slice_in_dim(block, 0, width, axis=dim), axis, backward)  5.61 us
  transfers between devices with their start and end apart: 9, of which 6 were waited for; matrix products, arithmetic and copies ran while one was open for 3% of the time, Pallas kernels for 0%

commit v1 on v0

v1 whole, which is shorter than its diff:
```python
import functools

import jax
import jax.numpy as jnp
from jax import lax
from jax.experimental import pallas as pl
from jax.experimental.pallas import tpu as pltpu
from jax.sharding import PartitionSpec as P

MESH = pl.DeviceIdType.MESH
SIDE = 16
DIRECTIONS = ((0, -1), (0, 1), (-1, 0), (1, 0), (-1, -1), (-1, 1), (1, -1), (1, 1))


def span(step, halo, size, inner):
    if step == 0:
        return pl.ds(0, size), pl.ds(inner, size)
    if step < 0:
        return pl.ds(0, halo), pl.ds(inner + size, halo)
    return pl.ds(size - halo, halo), pl.ds(inner - halo, halo)


def kernel(
    counts,
    f_ref, w1_ref, b1_ref, w2_ref, b2_ref, gain_ref, shift_ref, wd_ref, bd_ref,
    out_ref,
    xp, hid, cols_ref, w1, w2, wd, bd, pb, got, nf, ob,
    local_sem, fs, fr, hs, hr, ws, wr, vs, vr, bs, br, ps, pr, os_, or_,
):
    n_lat, n_lon, n_ch = counts
    rows, cols, width = f_ref.shape
    share = w1_ref.shape[1] // 5
    per = rows // n_ch
    lat, lon, ch = lax.axis_index("lat"), lax.axis_index("lon"), lax.axis_index("ch")
    half = lax.rem(lon, 2)
    partner = lon + 1 - 2 * half

    loads = [
        pltpu.make_async_copy(f_ref, xp.at[pl.ds(2, rows), pl.ds(SIDE, cols)], local_sem.at[0]),
        pltpu.make_async_copy(w1_ref, w1, local_sem.at[1]),
        pltpu.make_async_copy(w2_ref, w2, local_sem.at[2]),
        pltpu.make_async_copy(wd_ref, wd.at[ch], local_sem.at[3]),
        pltpu.make_async_copy(bd_ref, bd.at[ch], local_sem.at[4]),
    ]
    for load in loads:
        load.start()

    def present(dy, dx):
        ok = None
        for step, at, count in ((dy, lat, n_lat), (dx, lon, n_lon)):
            if step:
                here = (at > 0) if step < 0 else (at < count - 1)
                ok = here if ok is None else jnp.logical_and(ok, here)
        return ok

    barrier = pltpu.get_barrier_semaphore()
    expected = jnp.int32(n_ch - 1)
    for dy, dx in DIRECTIONS:
        there = present(dy, dx)
        expected = expected + jnp.where(there, 1, 0)

        @pl.when(there)
        def _(dy=dy, dx=dx):
            pl.semaphore_signal(barrier, inc=1, device_id=(lat + dy, lon + dx, ch), device_id_type=MESH)

    peers = [lax.rem(ch + k, n_ch) for k in range(n_ch)]
    for k in range(1, n_ch):
        pl.semaphore_signal(barrier, inc=1, device_id=(lat, lon, peers[k]), device_id_type=MESH)
    pl.semaphore_wait(barrier, expected)

    def halo(index, source, pad, inner, height, send, recv):
        dy, dx = DIRECTIONS[index]
        from_y, to_y = span(dy, height, rows, height)
        from_x, to_x = span(dx, SIDE, cols, SIDE)
        if inner:
            from_y = pl.ds(from_y.start + height, from_y.size)
            from_x = pl.ds(from_x.start + SIDE, from_x.size)
        return pltpu.make_async_remote_copy(
            source.at[from_y, from_x], pad.at[to_y, to_x], send.at[index], recv.at[index],
            device_id=(lat + dy, lon + dx, ch), device_id_type=MESH,
        )

    def feature_halo(index):
        return halo(index, f_ref, xp, False, 2, fs, fr)

    def hidden_halo(index):
        return halo(index, hid, hid, True, 4, hs, hr)

    def start(copy_of, indices):
        for index in indices:
            @pl.when(present(*DIRECTIONS[index]))
            def _(index=index):
                copy_of(index).start()

    def arrive(copy_of, indices):
        for index in indices:
            dy, dx = DIRECTIONS[index]

            @pl.when(present(-dy, -dx))
            def _(index=index):
                copy_of(index).wait_recv()

    def drain(copy_of, indices):
        for index in indices:
            @pl.when(present(*DIRECTIONS[index]))
            def _(index=index):
                copy_of(index).wait_send()

    start(feature_halo, range(8))

    def weight_send(k):
        part = pl.ds(2 * half, 2)
        return pltpu.make_async_remote_copy(
            wd_ref.at[part], wd.at[ch, part], ws.at[k], wr.at[k],
            device_id=(lat, lon, peers[k]), device_id_type=MESH,
        )

    def bias_send(k):
        return pltpu.make_async_remote_copy(
            bd_ref, bd.at[ch], bs.at[k], br.at[k],
            device_id=(lat, lon, peers[k]), device_id_type=MESH,
        )

    def weight_pass(k, which):
        origin = lax.rem(ch + n_ch - k, n_ch)
        part = pl.ds(2 * which, 2)
        return pltpu.make_async_remote_copy(
            wd.at[origin, part], wd.at[origin, part], vs.at[k], vr.at[k],
            device_id=(lat, partner, ch), device_id_type=MESH,
        )

    for k in range(1, n_ch):
        weight_send(k).start()
        bias_send(k).start()

    for pad, height in ((xp, 2), (hid, 4)):
        @pl.when(lat == 0)
        def _():
            pad[0:height] = jnp.zeros((height,) + pad.shape[1:], pad.dtype)

        @pl.when(lat == n_lat - 1)
        def _():
            pad[rows + height :] = jnp.zeros((height,) + pad.shape[1:], pad.dtype)

        @pl.when(lon == 0)
        def _():
            pad[:, 0:SIDE] = jnp.zeros((rows + 2 * height, SIDE, pad.shape[2]), pad.dtype)

        @pl.when(lon == n_lon - 1)
        def _():
            pad[:, cols + SIDE :] = jnp.zeros((rows + 2 * height, SIDE, pad.shape[2]), pad.dtype)

    span_cols = cols + 2 * SIDE

    def first(begin, count):
        total = None
        for tap in range(5):
            window = xp[pl.ds(begin + tap, count)].reshape(count * span_cols, width)
            term = lax.dot_general(
                window, w1[tap], (((1,), (1,)), ((), ())), preferred_element_type=jnp.float32
            )
            total = term if total is None else total + term
        total = total.reshape(count, span_cols, 5 * share)
        value = None
        for tap in range(5):
            low = SIDE - 2 + tap
            piece = total[:, low : low + cols, tap * share : (tap + 1) * share]
            value = piece if value is None else value + piece
        value = jax.nn.gelu(value + b1_ref[...][None], approximate=True)
        hid[pl.ds(begin + 4, count), pl.ds(SIDE, cols)] = value.astype(jnp.bfloat16)

    loads[0].wait()
    loads[1].wait()
    arrive(feature_halo, range(2))

    @pl.loop(0, (rows - 4) // 4)
    def _(step):
        first(2 + 4 * step, 4)

    arrive(feature_halo, range(2, 8))
    first(0, 2)
    first(rows - 2, 2)
    start(hidden_halo, range(8))

    for k in range(1, n_ch):
        weight_send(k).wait_recv()
        weight_pass(k, half).start()

    def spread(begin, count):
        pieces = [
            hid[pl.ds(begin, count), pl.ds(SIDE - 4 + 2 * tap, cols)] for tap in range(5)
        ]
        cols_ref[pl.ds(begin, count)] = jnp.concatenate(pieces, axis=2)

    def share_copy(block):
        return pltpu.make_async_remote_copy(
            pb.at[block], got.at[ch], ps.at[block], pr.at[ch],
            device_id=(lat, lon, block), device_id_type=MESH,
        )

    def second(block):
        total = None
        for tap in range(5):
            window = cols_ref[pl.ds(per * block + 2 * tap, per)].reshape(per * cols, 5 * share)
            term = jnp.dot(window, w2[tap], preferred_element_type=jnp.float32)
            total = term if total is None else total + term
        pb[block] = total.astype(jnp.bfloat16).reshape(per, cols, width)

        @pl.when(ch != block)
        def _():
            share_copy(block).start()

    arrive(hidden_halo, range(2))
    loads[2].wait()

    @pl.loop(0, rows // 4)
    def _(step):
        spread(4 + 4 * step, 4)

    inner = [b for b in range(n_ch) if per * b >= 4 and per * (b + 1) + 4 <= rows]
    for block in inner:
        second(block)
    arrive(hidden_halo, range(2, 8))
    spread(0, 4)
    spread(rows + 4, 4)
    for block in range(n_ch):
        if block not in inner:
            second(block)

    mixed = xp[pl.ds(2 + per * ch, per), pl.ds(SIDE, cols)].astype(jnp.float32) + b2_ref[...][None]
    mixed = mixed + pb[ch].astype(jnp.float32)
    for k in range(1, n_ch):
        origin = peers[k]
        pltpu.make_async_remote_copy(
            pb.at[0], got.at[origin], ps.at[0], pr.at[origin],
            device_id=(lat, lon, origin), device_id_type=MESH,
        ).wait_recv()
        mixed = mixed + got[origin].astype(jnp.float32)
    mean = jnp.sum(mixed, axis=2, keepdims=True) / width
    variance = jnp.sum(mixed * mixed, axis=2, keepdims=True) / width - mean * mean
    normed = (mixed - mean) * lax.rsqrt(variance + 1e-05) * gain_ref[...][None] + shift_ref[...][None]
    normed = normed.astype(jnp.bfloat16).astype(jnp.float32).reshape(per * cols, width)
    for part in range(width // 128):
        nf[part] = normed[:, part * 128 : (part + 1) * 128]

    loads[3].wait()
    loads[4].wait()
    for k in range(1, n_ch):
        bias_send(k).wait_recv()
        weight_pass(k, 1 - half).wait_recv()

    result = None
    for tap in range(4):
        i, j = tap // 2, tap % 2
        picked = [
            jnp.concatenate(
                [
                    nf[part, pl.ds((2 * r + i) * cols + j, cols // 2, stride=2), :]
                    for part in range(width // 128)
                ],
                axis=1,
            )
            for r in range(per // 2)
        ]
        window = jnp.concatenate(picked, axis=0).astype(jnp.bfloat16)
        term = lax.dot_general(
            window, wd[:, tap].reshape(n_ch * share, width), (((1,), (1,)), ((), ())),
            preferred_element_type=jnp.float32,
        )
        result = term if result is None else result + term
    for to in range(n_ch):
        piece = result[:, to * share : (to + 1) * share] + bd[to]
        ob[to] = piece.astype(jnp.bfloat16).reshape(per // 2, cols // 2, share)

    def out_copy(k):
        place = pl.ds((per // 2) * ch, per // 2)
        return pltpu.make_async_remote_copy(
            ob.at[peers[k]], out_ref.at[place], os_.at[k], or_.at[k],
            device_id=(lat, lon, peers[k]), device_id_type=MESH,
        )

    own = pltpu.make_async_copy(ob.at[ch], out_ref.at[pl.ds((per // 2) * ch, per // 2)], local_sem.at[5])
    for k in range(1, n_ch):
        out_copy(k).start()
    own.start()

    drain(feature_halo, range(8))
    drain(hidden_halo, range(8))
    for k in range(1, n_ch):
        weight_send(k).wait_send()
        bias_send(k).wait_send()
        weight_pass(k, half).wait_send()
    for block in range(n_ch):
        @pl.when(ch != block)
        def _(block=block):
            share_copy(block).wait_send()
    own.wait()
    for k in range(1, n_ch):
        out_copy(k).wait_send()
        origin = lax.rem(ch + n_ch - k, n_ch)
        pltpu.make_async_remote_copy(
            ob.at[0], out_ref.at[pl.ds((per // 2) * origin, per // 2)], os_.at[k], or_.at[k],
            device_id=(lat, lon, peers[k]), device_id_type=MESH,
        ).wait_recv()


def body(counts, features, w_first, bias_first, w_second, bias_second, norm_gain, norm_shift, w_down, bias_down):
    _, rows, cols, width = features.shape
    n_ch = counts[2]
    share = w_first.shape[3]
    per = rows // n_ch
    bf16, f32 = jnp.bfloat16, jnp.float32
    dma = pltpu.SemaphoreType.DMA
    anywhere = pl.BlockSpec(memory_space=pl.ANY)
    vmem = pl.BlockSpec(memory_space=pltpu.VMEM)
    result = pl.pallas_call(
        functools.partial(kernel, counts),
        out_shape=jax.ShapeDtypeStruct((rows // 2, cols // 2, share), bf16),
        in_specs=[anywhere, anywhere, vmem, anywhere, vmem, vmem, vmem, anywhere, vmem],
        out_specs=anywhere,
        scratch_shapes=[
            pltpu.VMEM((rows + 4, cols + 2 * SIDE, width), bf16),
            pltpu.VMEM((rows + 8, cols + 2 * SIDE, share), bf16),
            pltpu.VMEM((rows + 8, cols, 5 * share), bf16),
            pltpu.VMEM((5, 5 * share, width), bf16),
            pltpu.VMEM((5, 5 * share, width), bf16),
            pltpu.VMEM((n_ch, 4, share, width), bf16),
            pltpu.VMEM((n_ch, 1, share), f32),
            pltpu.VMEM((n_ch, per, cols, width), bf16),
            pltpu.VMEM((n_ch, per, cols, width), bf16),
            pltpu.VMEM((width // 128, per * cols, 128), f32),
            pltpu.VMEM((n_ch, per // 2, cols // 2, share), bf16),
            dma((6,)), dma((8,)), dma((8,)), dma((8,)), dma((8,)),
            dma((n_ch,)), dma((n_ch,)), dma((n_ch,)), dma((n_ch,)), dma((n_ch,)), dma((n_ch,)),
            dma((n_ch,)), dma((n_ch,)), dma((n_ch,)), dma((n_ch,)),
        ],
        compiler_params=pltpu.CompilerParams(
            collective_id=0, has_side_effects=True, vmem_limit_bytes=40 * 1024 * 1024
        ),
        cost_estimate=pl.CostEstimate(flops=1700000000, bytes_accessed=3000000, transcendentals=70000),
    )(
        features[0],
        jnp.transpose(w_first, (0, 1, 3, 2)).reshape(5, 5 * share, width),
        bias_first.reshape(1, share),
        w_second.reshape(5, 5 * share, width),
        bias_second.reshape(1, width),
        norm_gain.reshape(1, width),
        norm_shift.reshape(1, width),
        jnp.transpose(w_down, (0, 1, 3, 2)).reshape(4, share, width),
        bias_down.reshape(1, share),
    )
    return result[None]


def solution(mesh):
    placed = (
        P(None, "lat", "lon", None),
        P(None, None, None, "ch"),
        P("ch"),
        P(None, None, "ch", None),
        P(),
        P(),
        P(),
        P(None, None, None, "ch"),
        P("ch"),
    )
    counts = tuple(mesh.shape[name] for name in ("lat", "lon", "ch"))
    return jax.shard_map(
        functools.partial(body, counts),
        mesh=mesh, in_specs=placed, out_specs=P(None, "lat", "lon", "ch"), check_vma=False,
    )
```

time: 124 us -> 39.6 us (0.32)
  blocking collectives: 34.3 us -> 0 us
  Pallas kernels: 0 us -> 33.8 us
  waiting for transfers between devices: 29.4 us -> 0 us
  starting transfers between devices: 17.3 us -> 0 us
  matrix products: 16.7 us -> 0 us
  between operations: 14 us -> 0.02 us
  local copies, waits for them, and re-layouts: 10.2 us -> 5.59 us
    pallas_call x0 -> x1, Pallas kernels: none -> 33.8 us  [body(): pl.pallas_call(functools.partial(kernel, counts), out_shape=jax.ShapeDtyp...]
    unnamed x2 -> x0, waiting for transfers between devices: 20.2 us -> none
    all_gather x1 -> x0, blocking collectives: 18.5 us -> none  [body(): result = shrink(lax.all_gather(normed, 'ch', axis=3, tiled=True), w_down)]
    ppermute x8 -> x0, starting transfers between devices: 17.3 us -> none  [the longest x4 11.7 us: padded_2(): lax.ppermute(lax.slice_in_dim(block, block.shape[dim] - width, None, axis...]
    dot_general x51 -> x0, matrix products: 16.7 us -> none  [the longest x50 15.8 us: conv_taps(): jnp.einsum('bhwc,cd->bhwd', window, kernel[row_tap, col_tap], preferred_e...]
    psum x1 -> x0, blocking collectives: 15.8 us -> none  [body(): lax.psum((jnp.sum(mixed, axis=3), jnp.sum(mixed * mixed, axis=3)), 'ch')]
    ppermute x8 -> x0, waiting for transfers between devices: 9.13 us -> none  [the longest x4 8.68 us: padded_2(): lax.ppermute(lax.slice_in_dim(block, 0, width, axis=dim), axis, backward)]
    unnamed x23 -> x19, local copies, waits for them, and re-layouts: 7.54 us -> 5.59 us
  transfers between devices with their start and end apart: 9 -> 0, of which waited for: 6 -> 0; matrix products, arithmetic and copies ran while one was open for 3% -> 0% of each run, Pallas kernels for 0% -> 0%
where the time goes in v1:
time: 39.6 us; the launch traced here: 39.4 us
  Pallas kernels  33.8 us (85%)
  local copies, waits for them, and re-layouts  5.59 us (14%)
    pallas_call x1, Pallas kernels, body(): pl.pallas_call(functools.partial(kernel, counts), out_shape=jax.ShapeDtyp...  33.8 us
    unnamed x19, local copies, waits for them, and re-layouts  5.59 us

profile of v1, /device:TPU:0, one launch (start us, length us, event | category | flops | bytes accessed | tf_op | source)
XLA Modules:
  0.0 39.4 jit_solution(1500748880835486390)
XLA Ops:
  0.0 0.0 copy-start.8
  0.0 0.0 copy-start.5
  0.0 0.0 copy-start.6
  0.0 0.0 copy-start.4
  0.0 0.0 copy-start.7
  0.0 0.6 %copy-done.8 = f32[64]{0:T(128)S(1)} copy-done((f32[64]{0:T(128)S(1)}, f32[64]{0:T(128)}, u32[]{:S(2)}) %copy-start.8) | copy-done | bytes 280
  0.7 0.0 copy-done.5
  0.7 0.0 copy-done.6
  0.7 0.0 copy-done.4
  0.7 0.0 copy-done.7
  0.7 0.0 copy-start
  0.7 1.1 %copy-done = bf16[5,5,256,64]{2,3,1,0:T(8,128)(2,1)S(1)} copy-done((bf16[5,5,256,64]{2,3,1,0:T(8,128)(2,1)S(1)}, bf16[5,5,256,64]{2,3,1,0:T(8,128)(2,1)}, u32[]{:S(2)}) %copy-start) | copy-done | bytes 819224
  1.9 0.0 copy-start.1
  1.9 1.1 %copy-done.1 = bf16[5,5,64,256]{3,2,1,0:T(8,128)(2,1)S(1)} copy-done((bf16[5,5,64,256]{3,2,1,0:T(8,128)(2,1)S(1)}, bf16[5,5,64,256]{3,2,1,0:T(8,128)(2,1)}, u32[]{:S(2)}) %copy-start.1) | copy-done | bytes 819224
  3.0 0.0 copy-start.2
  3.0 1.0 %copy-done.2 = bf16[1,16,64,256]{3,2,1,0:T(8,128)(2,1)S(1)} copy-done((bf16[1,16,64,256]{3,2,1,0:T(8,128)(2,1)S(1)}, bf16[1,16,64,256]{3,2,1,0:T(8,128)(2,1)}, u32[]{:S(2)}) %copy-start.2) | copy-done | bytes 524312
  4.1 0.0 copy-start.3
  4.1 0.9 %copy-done.3 = bf16[2,2,256,64]{2,3,1,0:T(8,128)(2,1)S(1)} copy-done((bf16[2,2,256,64]{2,3,1,0:T(8,128)(2,1)S(1)}, bf16[2,2,256,64]{2,3,1,0:T(8,128)(2,1)}, u32[]{:S(2)}) %copy-start.3) | copy-done | bytes 131096
  5.0 33.8 %shard_map.91 = bf16[8,32,64]{2,1,0:T(8,128)(2,1)S(1)} custom-call(bf16[16,64,256]{2,1,0:T(8,128)(2,1)S(1)} %bitcast.17, bf16[5,320,256]{2,1,0:T(8,128)(2,1)S(1)} %bitcast.15, f32[1,64]{1,0:T(1,128)S(1)} %bitcast.22, bf16[5,320,256]{2,1,0:T(8,128)(2,1)S(1)} %bitcast.16, f32[1,256]{1,0:T(1,128)S(1)} %bitcast.19, f32[1,256]{1,0:T(1,128)S(1)} %bitcast.20, ...), custom_call_target="tpu_custom_call" | custom-call | flops 1700000000 | bytes 3000000 | tf_op jit(solution)/shard_map/pallas_call | solution.py:316
  38.7 0.6 %copy.11 = bf16[1,8,32,64]{3,2,1,0:T(8,128)(2,1)} copy(bf16[1,8,32,64]{3,2,1,0:T(8,128)(2,1)S(1)} %bitcast.14) | data formatting | bytes 65536
Async XLA Ops:
  0.0 0.7 %copy-start.8 = (f32[64]{0:T(128)S(1)}, f32[64]{0:T(128)}, u32[]{:S(2)}) copy-start(f32[64]{0:T(128)} %param.17) | copy-start | bytes 772
  0.0 0.7 %copy-start.5 = (f32[256]{0:T(256)S(1)}, f32[256]{0:T(256)}, u32[]{:S(2)}) copy-start(f32[256]{0:T(256)} %param.14) | copy-start | bytes 3076
  0.0 0.7 %copy-start.6 = (f32[256]{0:T(256)S(1)}, f32[256]{0:T(256)}, u32[]{:S(2)}) copy-start(f32[256]{0:T(256)} %param.15) | copy-start | bytes 3076
  0.0 0.7 %copy-start.4 = (f32[256]{0:T(256)S(1)}, f32[256]{0:T(256)}, u32[]{:S(2)}) copy-start(f32[256]{0:T(256)} %param.13) | copy-start | bytes 3076
  0.0 0.7 %copy-start.7 = (f32[64]{0:T(128)S(1)}, f32[64]{0:T(128)}, u32[]{:S(2)}) copy-start(f32[64]{0:T(128)} %param.11) | copy-start | bytes 772
  0.7 1.1 %copy-start = (bf16[5,5,256,64]{2,3,1,0:T(8,128)(2,1)S(1)}, bf16[5,5,256,64]{2,3,1,0:T(8,128)(2,1)}, u32[]{:S(2)}) copy-start(bf16[5,5,256,64]{2,3,1,0:T(8,128)(2,1)} %param.10) | copy-start | bytes 2457604
  1.9 1.1 %copy-start.1 = (bf16[5,5,64,256]{3,2,1,0:T(8,128)(2,1)S(1)}, bf16[5,5,64,256]{3,2,1,0:T(8,128)(2,1)}, u32[]{:S(2)}) copy-start(bf16[5,5,64,256]{3,2,1,0:T(8,128)(2,1)} %param.12) | copy-start | bytes 2457604
  3.0 1.0 %copy-start.2 = (bf16[1,16,64,256]{3,2,1,0:T(8,128)(2,1)S(1)}, bf16[1,16,64,256]{3,2,1,0:T(8,128)(2,1)}, u32[]{:S(2)}) copy-start(bf16[1,16,64,256]{3,2,1,0:T(8,128)(2,1)} %param.9) | copy-start | bytes 1572868
  4.1 0.9 %copy-start.3 = (bf16[2,2,256,64]{2,3,1,0:T(8,128)(2,1)S(1)}, bf16[2,2,256,64]{2,3,1,0:T(8,128)(2,1)}, u32[]{:S(2)}) copy-start(bf16[2,2,256,64]{2,3,1,0:T(8,128)(2,1)} %param.16) | copy-start | bytes 393220

commit v2 on v1

--- a/solution.py
+++ b/solution.py
@@ -335,7 +335,7 @@
             dma((n_ch,)), dma((n_ch,)), dma((n_ch,)), dma((n_ch,)),
         ],
         compiler_params=pltpu.CompilerParams(
-            collective_id=0, has_side_effects=True, vmem_limit_bytes=40 * 1024 * 1024
+            collective_id=0, has_side_effects=True, vmem_limit_bytes=60 * 1024 * 1024
         ),
         cost_estimate=pl.CostEstimate(flops=1700000000, bytes_accessed=3000000, transcendentals=70000),
     )(

time: 39.6 us -> 36.2 us (0.914)
  local copies, waits for them, and re-layouts: 5.59 us -> 1.47 us
  Pallas kernels: 33.8 us -> 34.5 us
    unnamed x19 -> x1, local copies, waits for them, and re-layouts: 5.59 us -> 1.47 us
    pallas_call x1, Pallas kernels: 33.8 us -> 34.5 us  [body(): pl.pallas_call(functools.partial(kernel, counts), out_shape=jax.ShapeDtyp...]
where the time goes in v2:
time: 36.2 us; the launch traced here: 36 us
  Pallas kernels  34.5 us (95%)
  local copies, waits for them, and re-layouts  1.47 us (4%)
    pallas_call x1, Pallas kernels, body(): pl.pallas_call(functools.partial(kernel, counts), out_shape=jax.ShapeDtyp...  34.5 us
    unnamed x1, local copies, waits for them, and re-layouts  1.47 us

profile of v2, /device:TPU:0, one launch (start us, length us, event | category | flops | bytes accessed | tf_op | source)
XLA Modules:
  0.0 36.0 jit_solution(12461939788436473269)
XLA Ops:
  0.0 34.5 %shard_map.91 = bf16[8,32,64]{2,1,0:T(8,128)(2,1)} custom-call(bf16[16,64,256]{2,1,0:T(8,128)(2,1)} %bitcast.17, bf16[5,320,256]{2,1,0:T(8,128)(2,1)} %bitcast.15, f32[1,64]{1,0:T(1,128)} %bitcast.22, bf16[5,320,256]{2,1,0:T(8,128)(2,1)} %bitcast.16, f32[1,256]{1,0:T(1,128)} %bitcast.19, f32[1,256]{1,0:T(1,128)} %bitcast.20, f32[1,256]{1,0:T(1,128)} %bitcast.21, ...), custom_call_target="tpu_custom_call" | custom-call | flops 1700000000 | bytes 3000000 | tf_op jit(solution)/shard_map/pallas_call | solution.py:316
  34.5 1.5 %copy.11 = bf16[1,8,32,64]{3,2,1,0:T(8,128)(2,1)} copy(bf16[1,8,32,64]{3,2,1,0:T(8,128)(2,1)} %bitcast.14) | data formatting | bytes 65536

commit v3 on v2

--- a/solution.py
+++ b/solution.py
@@ -198,16 +198,14 @@
             device_id=(lat, lon, block), device_id_type=MESH,
         )
 
-    def second(block):
+    def second(block, send):
         total = None
         for tap in range(5):
             window = cols_ref[pl.ds(per * block + 2 * tap, per)].reshape(per * cols, 5 * share)
             term = jnp.dot(window, w2[tap], preferred_element_type=jnp.float32)
             total = term if total is None else total + term
         pb[block] = total.astype(jnp.bfloat16).reshape(per, cols, width)
-
-        @pl.when(ch != block)
-        def _():
+        if send:
             share_copy(block).start()
 
     arrive(hidden_halo, range(2))
@@ -217,15 +215,18 @@
     def _(step):
         spread(4 + 4 * step, 4)
 
-    inner = [b for b in range(n_ch) if per * b >= 4 and per * (b + 1) + 4 <= rows]
-    for block in inner:
-        second(block)
+    middle = n_ch // 2
+    low = ch < middle
+    across = jnp.where(low, middle, middle - 1)
+    outer = jnp.where(low, n_ch - 1, 0)
+    beside = jnp.where(low, middle - 1 - ch, n_ch + middle - 1 - ch)
+    second(across, True)
     arrive(hidden_halo, range(2, 8))
     spread(0, 4)
     spread(rows + 4, 4)
-    for block in range(n_ch):
-        if block not in inner:
-            second(block)
+    second(outer, True)
+    second(beside, True)
+    second(ch, False)
 
     mixed = xp[pl.ds(2 + per * ch, per), pl.ds(SIDE, cols)].astype(jnp.float32) + b2_ref[...][None]
     mixed = mixed + pb[ch].astype(jnp.float32)
@@ -290,10 +291,8 @@
         weight_send(k).wait_send()
         bias_send(k).wait_send()
         weight_pass(k, half).wait_send()
-    for block in range(n_ch):
-        @pl.when(ch != block)
-        def _(block=block):
-            share_copy(block).wait_send()
+    for block in (across, outer, beside):
+        share_copy(block).wait_send()
     own.wait()
     for k in range(1, n_ch):
         out_copy(k).wait_send()

time: 36.2 us -> 36 us (level)
  no operation moved by 1% of the time
where the time goes in v3:
time: 36 us; the launch traced here: 35.8 us
  Pallas kernels  34.3 us (95%)
  local copies, waits for them, and re-layouts  1.47 us (4%)
    pallas_call x1, Pallas kernels, body(): pl.pallas_call(functools.partial(kernel, counts), out_shape=jax.ShapeDtyp...  34.3 us
    unnamed x1, local copies, waits for them, and re-layouts  1.47 us

profile of v3, /device:TPU:0, one launch (start us, length us, event | category | flops | bytes accessed | tf_op | source)
XLA Modules:
  0.0 35.8 jit_solution(18359859263184177638)
XLA Ops:
  0.0 34.3 %shard_map.91 = bf16[8,32,64]{2,1,0:T(8,128)(2,1)} custom-call(bf16[16,64,256]{2,1,0:T(8,128)(2,1)} %bitcast.17, bf16[5,320,256]{2,1,0:T(8,128)(2,1)} %bitcast.15, f32[1,64]{1,0:T(1,128)} %bitcast.22, bf16[5,320,256]{2,1,0:T(8,128)(2,1)} %bitcast.16, f32[1,256]{1,0:T(1,128)} %bitcast.19, f32[1,256]{1,0:T(1,128)} %bitcast.20, f32[1,256]{1,0:T(1,128)} %bitcast.21, ...), custom_call_target="tpu_custom_call" | custom-call | flops 1700000000 | bytes 3000000 | tf_op jit(solution)/shard_map/pallas_call | solution.py:315
  34.3 1.5 %copy.11 = bf16[1,8,32,64]{3,2,1,0:T(8,128)(2,1)} copy(bf16[1,8,32,64]{3,2,1,0:T(8,128)(2,1)} %bitcast.14) | data formatting | bytes 65536

commit v4 on v3

--- a/solution.py
+++ b/solution.py
@@ -24,8 +24,8 @@
     counts,
     f_ref, w1_ref, b1_ref, w2_ref, b2_ref, gain_ref, shift_ref, wd_ref, bd_ref,
     out_ref,
-    xp, hid, cols_ref, w1, w2, wd, bd, pb, got, nf, ob,
-    local_sem, fs, fr, hs, hr, ws, wr, vs, vr, bs, br, ps, pr, os_, or_,
+    xp, hid, cols_ref, w1, w2, wd, bd, pb, got, via, nf, ob,
+    local_sem, fs, fr, hs, hr, ws, wr, vs, vr, bs, br, ps, pr, rs, rr, os_, or_,
 ):
     n_lat, n_lon, n_ch = counts
     rows, cols, width = f_ref.shape
@@ -192,21 +192,13 @@
         ]
         cols_ref[pl.ds(begin, count)] = jnp.concatenate(pieces, axis=2)
 
-    def share_copy(block):
-        return pltpu.make_async_remote_copy(
-            pb.at[block], got.at[ch], ps.at[block], pr.at[ch],
-            device_id=(lat, lon, block), device_id_type=MESH,
-        )
-
-    def second(block, send):
+    def second(block):
         total = None
         for tap in range(5):
             window = cols_ref[pl.ds(per * block + 2 * tap, per)].reshape(per * cols, 5 * share)
             term = jnp.dot(window, w2[tap], preferred_element_type=jnp.float32)
             total = term if total is None else total + term
         pb[block] = total.astype(jnp.bfloat16).reshape(per, cols, width)
-        if send:
-            share_copy(block).start()
 
     arrive(hidden_halo, range(2))
     loads[2].wait()
@@ -220,18 +212,53 @@
     across = jnp.where(low, middle, middle - 1)
     outer = jnp.where(low, n_ch - 1, 0)
     beside = jnp.where(low, middle - 1 - ch, n_ch + middle - 1 - ch)
-    second(across, True)
+    edge = jnp.logical_or(ch == 0, ch == n_ch - 1)
+    inside = jnp.logical_not(edge)
+    far = (across, outer)
+
+    def relay_copy(n):
+        return pltpu.make_async_remote_copy(
+            pb.at[far[n]], via.at[n], rs.at[n], rr.at[n],
+            device_id=(lat, lon, beside), device_id_type=MESH,
+        )
+
+    def share_copy(n, block):
+        return pltpu.make_async_remote_copy(
+            pb.at[block], got.at[ch], ps.at[n], pr.at[ch],
+            device_id=(lat, lon, block), device_id_type=MESH,
+        )
+
+    second(across)
+
+    @pl.when(edge)
+    def _():
+        relay_copy(0).start()
+
     arrive(hidden_halo, range(2, 8))
     spread(0, 4)
     spread(rows + 4, 4)
-    second(outer, True)
-    second(beside, True)
-    second(ch, False)
+    second(outer)
+
+    @pl.when(edge)
+    def _():
+        relay_copy(1).start()
+
+    second(beside)
+    share_copy(2, beside).start()
+
+    @pl.when(inside)
+    def _():
+        for n in range(2):
+            relay_copy(n).wait_recv()
+            both = pb[far[n]].astype(jnp.float32) + via[n].astype(jnp.float32)
+            pb[far[n]] = both.astype(jnp.bfloat16)
+            share_copy(n, far[n]).start()
+
+    second(ch)
 
     mixed = xp[pl.ds(2 + per * ch, per), pl.ds(SIDE, cols)].astype(jnp.float32) + b2_ref[...][None]
     mixed = mixed + pb[ch].astype(jnp.float32)
-    for k in range(1, n_ch):
-        origin = peers[k]
+    for origin in (beside, across):
         pltpu.make_async_remote_copy(
             pb.at[0], got.at[origin], ps.at[0], pr.at[origin],
             device_id=(lat, lon, origin), device_id_type=MESH,
@@ -291,8 +318,15 @@
         weight_send(k).wait_send()
         bias_send(k).wait_send()
         weight_pass(k, half).wait_send()
-    for block in (across, outer, beside):
-        share_copy(block).wait_send()
+    share_copy(2, beside).wait_send()
+    for n in range(2):
+        @pl.when(edge)
+        def _(n=n):
+            relay_copy(n).wait_send()
+
+        @pl.when(inside)
+        def _(n=n):
+            share_copy(n, far[n]).wait_send()
     own.wait()
     for k in range(1, n_ch):
         out_copy(k).wait_send()
@@ -327,11 +361,12 @@
             pltpu.VMEM((n_ch, 1, share), f32),
             pltpu.VMEM((n_ch, per, cols, width), bf16),
             pltpu.VMEM((n_ch, per, cols, width), bf16),
+            pltpu.VMEM((2, per, cols, width), bf16),
             pltpu.VMEM((width // 128, per * cols, 128), f32),
             pltpu.VMEM((n_ch, per // 2, cols // 2, share), bf16),
             dma((6,)), dma((8,)), dma((8,)), dma((8,)), dma((8,)),
             dma((n_ch,)), dma((n_ch,)), dma((n_ch,)), dma((n_ch,)), dma((n_ch,)), dma((n_ch,)),
-            dma((n_ch,)), dma((n_ch,)), dma((n_ch,)), dma((n_ch,)),
+            dma((n_ch,)), dma((n_ch,)), dma((2,)), dma((2,)), dma((n_ch,)), dma((n_ch,)),
         ],
         compiler_params=pltpu.CompilerParams(
             collective_id=0, has_side_effects=True, vmem_limit_bytes=60 * 1024 * 1024

time: 36 us -> 35.6 us (0.989)
  Pallas kernels: 34.3 us -> 33.9 us
    pallas_call x1, Pallas kernels: 34.3 us -> 33.9 us  [body(): pl.pallas_call(functools.partial(kernel, counts), out_shape=jax.ShapeDtyp...]
where the time goes in v4:
time: 35.6 us; the launch traced here: 35.4 us
  Pallas kernels  33.9 us (95%)
  local copies, waits for them, and re-layouts  1.47 us (4%)
    pallas_call x1, Pallas kernels, body(): pl.pallas_call(functools.partial(kernel, counts), out_shape=jax.ShapeDtyp...  33.9 us
    unnamed x1, local copies, waits for them, and re-layouts  1.47 us

profile of v4, /device:TPU:0, one launch (start us, length us, event | category | flops | bytes accessed | tf_op | source)
XLA Modules:
  0.0 35.4 jit_solution(1083919274246185210)
XLA Ops:
  0.0 33.9 %shard_map.91 = bf16[8,32,64]{2,1,0:T(8,128)(2,1)} custom-call(bf16[16,64,256]{2,1,0:T(8,128)(2,1)} %bitcast.17, bf16[5,320,256]{2,1,0:T(8,128)(2,1)} %bitcast.15, f32[1,64]{1,0:T(1,128)} %bitcast.22, bf16[5,320,256]{2,1,0:T(8,128)(2,1)} %bitcast.16, f32[1,256]{1,0:T(1,128)} %bitcast.19, f32[1,256]{1,0:T(1,128)} %bitcast.20, f32[1,256]{1,0:T(1,128)} %bitcast.21, ...), custom_call_target="tpu_custom_call" | custom-call | flops 1700000000 | bytes 3000000 | tf_op jit(solution)/shard_map/pallas_call | solution.py:349
  33.9 1.5 %copy.11 = bf16[1,8,32,64]{3,2,1,0:T(8,128)(2,1)} copy(bf16[1,8,32,64]{3,2,1,0:T(8,128)(2,1)} %bitcast.14) | data formatting | bytes 65536

commit v5 on v4

--- a/solution.py
+++ b/solution.py
@@ -182,10 +182,6 @@
     first(rows - 2, 2)
     start(hidden_halo, range(8))
 
-    for k in range(1, n_ch):
-        weight_send(k).wait_recv()
-        weight_pass(k, half).start()
-
     def spread(begin, count):
         pieces = [
             hid[pl.ds(begin, count), pl.ds(SIDE - 4 + 2 * tap, cols)] for tap in range(5)
@@ -216,15 +212,23 @@
     inside = jnp.logical_not(edge)
     far = (across, outer)
 
-    def relay_copy(n):
-        return pltpu.make_async_remote_copy(
-            pb.at[far[n]], via.at[n], rs.at[n], rr.at[n],
+    halves = [pl.ds(part * (per // 2), per // 2) for part in range(2)]
+
+    def relay_copy(n, part):
+        return pltpu.make_async_remote_copy(
+            pb.at[far[n], halves[part]], via.at[n, halves[part]], rs.at[2 * n + part], rr.at[2 * n + part],
             device_id=(lat, lon, beside), device_id_type=MESH,
         )
 
-    def share_copy(n, block):
-        return pltpu.make_async_remote_copy(
-            pb.at[block], got.at[ch], ps.at[n], pr.at[ch],
+    def far_copy(n, part):
+        return pltpu.make_async_remote_copy(
+            pb.at[far[n], halves[part]], got.at[ch, halves[part]], ps.at[2 * n + part], pr.at[ch],
+            device_id=(lat, lon, far[n]), device_id_type=MESH,
+        )
+
+    def share_copy(block):
+        return pltpu.make_async_remote_copy(
+            pb.at[block], got.at[ch], ps.at[4], pr.at[ch],
             device_id=(lat, lon, block), device_id_type=MESH,
         )
 
@@ -232,7 +236,8 @@
 
     @pl.when(edge)
     def _():
-        relay_copy(0).start()
+        relay_copy(0, 0).start()
+        relay_copy(0, 1).start()
 
     arrive(hidden_halo, range(2, 8))
     spread(0, 4)
@@ -241,20 +246,27 @@
 
     @pl.when(edge)
     def _():
-        relay_copy(1).start()
+        relay_copy(1, 0).start()
+        relay_copy(1, 1).start()
 
     second(beside)
-    share_copy(2, beside).start()
+    share_copy(beside).start()
 
     @pl.when(inside)
     def _():
         for n in range(2):
-            relay_copy(n).wait_recv()
-            both = pb[far[n]].astype(jnp.float32) + via[n].astype(jnp.float32)
-            pb[far[n]] = both.astype(jnp.bfloat16)
-            share_copy(n, far[n]).start()
+            for part in range(2):
+                relay_copy(n, part).wait_recv()
+                here = halves[part]
+                both = pb[far[n], here].astype(jnp.float32) + via[n, here].astype(jnp.float32)
+                pb[far[n], here] = both.astype(jnp.bfloat16)
+                far_copy(n, part).start()
 
     second(ch)
+    for k in range(1, n_ch):
+        weight_send(k).wait_recv()
+        weight_pass(k, half).start()
+
 
     mixed = xp[pl.ds(2 + per * ch, per), pl.ds(SIDE, cols)].astype(jnp.float32) + b2_ref[...][None]
     mixed = mixed + pb[ch].astype(jnp.float32)
@@ -318,15 +330,17 @@
         weight_send(k).wait_send()
         bias_send(k).wait_send()
         weight_pass(k, half).wait_send()
-    share_copy(2, beside).wait_send()
+    share_copy(beside).wait_send()
     for n in range(2):
         @pl.when(edge)
         def _(n=n):
-            relay_copy(n).wait_send()
+            relay_copy(n, 0).wait_send()
+            relay_copy(n, 1).wait_send()
 
         @pl.when(inside)
         def _(n=n):
-            share_copy(n, far[n]).wait_send()
+            far_copy(n, 0).wait_send()
+            far_copy(n, 1).wait_send()
     own.wait()
     for k in range(1, n_ch):
         out_copy(k).wait_send()
@@ -366,7 +380,7 @@
             pltpu.VMEM((n_ch, per // 2, cols // 2, share), bf16),
             dma((6,)), dma((8,)), dma((8,)), dma((8,)), dma((8,)),
             dma((n_ch,)), dma((n_ch,)), dma((n_ch,)), dma((n_ch,)), dma((n_ch,)), dma((n_ch,)),
-            dma((n_ch,)), dma((n_ch,)), dma((2,)), dma((2,)), dma((n_ch,)), dma((n_ch,)),
+            dma((5,)), dma((n_ch,)), dma((4,)), dma((4,)), dma((n_ch,)), dma((n_ch,)),
         ],
         compiler_params=pltpu.CompilerParams(
             collective_id=0, has_side_effects=True, vmem_limit_bytes=60 * 1024 * 1024

time: 35.6 us -> 34.5 us (0.969)
  Pallas kernels: 33.9 us -> 32.8 us
    pallas_call x1, Pallas kernels: 33.9 us -> 32.8 us  [body(): pl.pallas_call(functools.partial(kernel, counts), out_shape=jax.ShapeDtyp...]
where the time goes in v5:
time: 34.5 us; the launch traced here: 34.3 us
  Pallas kernels  32.8 us (95%)
  local copies, waits for them, and re-layouts  1.47 us (4%)
    pallas_call x1, Pallas kernels, body(): pl.pallas_call(functools.partial(kernel, counts), out_shape=jax.ShapeDtyp...  32.8 us
    unnamed x1, local copies, waits for them, and re-layouts  1.47 us

profile of v5, /device:TPU:0, one launch (start us, length us, event | category | flops | bytes accessed | tf_op | source)
XLA Modules:
  0.0 34.3 jit_solution(9609441841529664318)
XLA Ops:
  0.0 32.8 %shard_map.91 = bf16[8,32,64]{2,1,0:T(8,128)(2,1)} custom-call(bf16[16,64,256]{2,1,0:T(8,128)(2,1)} %bitcast.17, bf16[5,320,256]{2,1,0:T(8,128)(2,1)} %bitcast.15, f32[1,64]{1,0:T(1,128)} %bitcast.22, bf16[5,320,256]{2,1,0:T(8,128)(2,1)} %bitcast.16, f32[1,256]{1,0:T(1,128)} %bitcast.19, f32[1,256]{1,0:T(1,128)} %bitcast.20, f32[1,256]{1,0:T(1,128)} %bitcast.21, ...), custom_call_target="tpu_custom_call" | custom-call | flops 1700000000 | bytes 3000000 | tf_op jit(solution)/shard_map/pallas_call | solution.py:363
  32.8 1.5 %copy.11 = bf16[1,8,32,64]{3,2,1,0:T(8,128)(2,1)} copy(bf16[1,8,32,64]{3,2,1,0:T(8,128)(2,1)} %bitcast.14) | data formatting | bytes 65536
